TPU v7x, 512 devices: a whole 4x8x8 slice. The times are simulated.
512 devices in a mesh: language: 8 (over y_hi, core), fsdp: 64 (over y_lo, x, z).
Axes of the slice: x: 4, y: 8 (y_hi: 4, y_lo: 2; y = y_hi * 2 + y_lo), z: 8, core: 2. Of those that a mesh axis runs over, the one named last changes fastest.
Arguments:
- hidden: bfloat16 [16, 8192, 5120], P('language', 'fsdp'), may hold values from -60 to 60
- latent_grad: bfloat16 [16, 8192, 64], P('language', 'fsdp'), may hold values from -0.15625 to 0.15625
- lang_ids: int32 [16], P('language'), may hold values from 0 to 15, each once
- old_weights: float32 [16], replicated, may hold values from 0.02 to 0.2
- param: float32 [5120, 64], P('fsdp'), may hold values from -6 to 6
- first_moment: float32 [5120, 64], P('fsdp'), may hold values from -6 to 6
- second_moment: float32 [5120, 64], P('fsdp'), may hold values from 0.25 to 4
Outputs:
- new_param: float32 [5120, 64], P('fsdp')
- new_first: float32 [5120, 64], P('fsdp')
- new_second: float32 [5120, 64], P('fsdp')
- new_logweights: float32 [16], replicated
Inputs may be any that keep to these rules, and one draw needn't show every extreme that they name: `lang_ids`: each id appears in exactly one slot.
All inputs are finite; a program needn't handle non-finite values.
Results may differ from a plain program's by a relative error of at most 0.0003.
Values may be sent and summed in bfloat16 or wider, within the bound.
A program may use at most 64 MiB of HBM per device.

v0:
```python
import jax
import jax.numpy as jnp
from jax import lax
from jax.sharding import PartitionSpec as P

STEP = 100


def log_weights(by_lang, square, old_weights):
    logits = jnp.log(old_weights) + old_weights.shape[0] * (by_lang / (square + 1e-06))
    return logits - jnp.log(jnp.sum(jnp.exp(logits)))


def local(hidden, latent_grad, lang_ids, old_weights, param, first_moment, second_moment):
    langs = old_weights.shape[0]
    slot_grad = lax.psum_scatter(
        jnp.einsum("ltd,ltr->dlr", hidden, latent_grad, preferred_element_type=jnp.float32),
        "fsdp",
        scatter_dimension=0,
        tiled=True,
    )
    onehot = (lang_ids[:, None] == jnp.arange(langs, dtype=jnp.int32)[None, :]).astype(jnp.float32)
    total = lax.psum(jnp.sum(slot_grad, axis=1), "language")
    dots = jnp.einsum("dlr,dr->l", slot_grad, total, precision=lax.Precision.HIGHEST)
    leader = (lax.axis_index("language") == 0).astype(jnp.float32)
    square_part = jnp.sum(total * total) * leader
    by_lang_part = jnp.dot(dots, onehot, precision=lax.Precision.HIGHEST)
    by_lang, square = lax.psum((by_lang_part, square_part), ("language", "fsdp"))
    new_logweights = log_weights(by_lang, square, old_weights)
    weights = jnp.exp(new_logweights)
    slot_weight = jnp.dot(onehot, weights, precision=lax.Precision.HIGHEST)
    local_update = jnp.einsum("l,dlr->dr", slot_weight, slot_grad, precision=lax.Precision.HIGHEST)
    update = lax.psum(local_update, "language")
    new_first = 0.9 * first_moment + 0.1 * update
    new_second = 0.95 * second_moment + 0.05 * update * update
    first_hat = new_first / (1.0 - 0.9**STEP)
    second_hat = new_second / (1.0 - 0.95**STEP)
    new_param = param - 0.02 * (first_hat / (jnp.sqrt(second_hat) + 1e-08) + 0.1 * param)
    return (new_param, new_first, new_second, new_logweights)


def solution(mesh):
    placed = (
        P("language", "fsdp", None),
        P("language", "fsdp", None),
        P("language"),
        P(),
        P("fsdp", None),
        P("fsdp", None),
        P("fsdp", None),
    )
    return jax.shard_map(
        local,
        mesh=mesh,
        in_specs=placed,
        out_specs=(P("fsdp", None), P("fsdp", None), P("fsdp", None), P()),
        check_vma=False,
    )
```

profile of v0, /device:TPU:2, one launch (start us, length us, event | category | flops | bytes accessed | tf_op | source)
XLA Modules:
  0.0 505.8 jit_solution(7632736756905314304)
XLA Ops:
  7.2 0.0 copy-start
  7.2 0.0 reduce-scatter.4.cloned.1.call-start
  7.2 1.7 copy-done
  8.9 2.8 fusion.7
  11.7 3.2 copy.16
  14.9 0.0 copy-start.5
  14.9 0.0 copy-start.4
  14.9 0.0 copy-start.1
  14.9 0.0 copy-start.2
  14.9 0.0 copy-start.3
  14.9 0.0 reduce-scatter.4.cloned.1.call-update
  15.0 310.9 %reduce-scatter.4.cloned.1.call-done = f32[80,128]{1,0:T(8,128)} async-done(((f32[5120,128]{1,0:T(8,128)}), f32[80,128]{1,0:T(8,128)}) %reduce-scatter.4.cloned.1.call-update) | async-done | bytes 40976
  325.9 0.9 copy.17
  326.8 27.2 %psum.28 = f32[80,64]{0,1:T(8,128)S(1)} all-reduce(f32[80,64]{0,1:T(8,128)S(1)} %reduce_sum.27), channel_id=1, replica_groups=mesh['language'=8,'fsdp'=64] {'language'}, use_global_device_ids=true, to_apply=%region_2.0 | all-reduce | flops 5120 | bytes 40960 | tf_op jit(solution)/shard_map/psum | solution.py:23
  354.0 0.6 multiply_reduce_fusion
  354.6 0.7 convolution_bitcast_fusion.2
  355.3 0.0 copy-done.5
  355.3 0.2 convolution_bitcast_fusion.1
  356.1 111.2 %all-reduce = (f32[16]{0:T(128)S(1)}, f32[]{:T(128)}) all-reduce(f32[16]{0:T(128)S(1)} %convolution_bitcast_fusion.1, f32[]{:T(128)S(6)} %mul.45), channel_id=1, replica_groups=mesh['language'=8,'fsdp'=64] {'language','fsdp'}, use_global_device_ids=true, to_apply=%region_3.0 | all-reduce | flops 17 | bytes 136 | tf_op jit(solution)/shard_map/psum | solution.py:28
  468.0 0.0 copy-done.4
  468.0 0.6 exponential_reduce_fusion
  469.3 0.0 copy-start.6
  469.3 0.2 convolution_bitcast_fusion
  469.5 0.4 fusion
  469.9 28.4 %psum.31 = f32[80,64]{0,1:T(8,128)S(1)} all-reduce(f32[80,64]{0,1:T(8,128)S(1)} %bitcast.34), channel_id=1, replica_groups=mesh['language'=8,'fsdp'=64] {'language'}, use_global_device_ids=true, to_apply=%region_7.0 | all-reduce | flops 5120 | bytes 40960 | tf_op jit(solution)/shard_map/psum | solution.py:33
  498.3 0.0 copy-done.1
  498.3 0.0 copy-done.2
  498.3 0.0 copy-done.3
  498.3 0.7 multiply_subtract_fusion
  499.0 0.0 copy-done.6
  (2 shorter events, 0.0 us)
Async XLA Ops:
  7.2 1.7 copy-start
  7.2 318.7 %reduce-scatter.4.cloned.1.call-start = ((), (), s32[]{:S(2)}) async-start(), calls=%async_computation.1 | async-start | bytes 2662400
  14.9 340.3 %copy-start.5 = (s32[2]{0:T(128)S(1)}, s32[2]{0:T(128)}, u32[]{:S(2)}) copy-start(s32[2]{0:T(128)} %param.9) | copy-start | bytes 28
  14.9 453.1 %copy-start.4 = (f32[16]{0:T(128)S(1)}, f32[16]{0:T(128)}, u32[]{:S(2)}) copy-start(f32[16]{0:T(128)} %param.10) | copy-start | bytes 196
  14.9 483.4 %copy-start.1 = (f32[80,64]{0,1:T(8,128)S(1)}, f32[80,64]{0,1:T(8,128)}, u32[]{:S(2)}) copy-start(f32[80,64]{0,1:T(8,128)} %param.11) | copy-start | bytes 61444
  14.9 483.4 %copy-start.2 = (f32[80,64]{0,1:T(8,128)S(1)}, f32[80,64]{0,1:T(8,128)}, u32[]{:S(2)}) copy-start(f32[80,64]{0,1:T(8,128)} %param.12) | copy-start | bytes 61444
  14.9 483.4 %copy-start.3 = (f32[80,64]{0,1:T(8,128)S(1)}, f32[80,64]{0,1:T(8,128)}, u32[]{:S(2)}) copy-start(f32[80,64]{0,1:T(8,128)} %param.13) | copy-start | bytes 61444
  469.3 29.7 %copy-start.6 = (f32[16]{0:T(128)}, f32[16]{0:T(128)S(1)}, u32[]{:S(2)}) copy-start(f32[16]{0:T(128)S(1)} %broadcast_subtract_fusion) | copy-start | bytes 196
Sparse Core Ops, SparseCore 0:
  15.1 310.7 reduce-scatter.3
where the time goes:
time: 506 us
  waiting for transfers between devices  311 us (61%)
  blocking collectives  167 us (33%)
  between operations  16.1 us (3%)
  local copies, waits for them, and re-layouts  5.81 us (1%)
    unnamed x2, waiting for transfers between devices  311 us
    psum x1, blocking collectives, local(): lax.psum((by_lang_part, square_part), ('language', 'fsdp'))  111 us
    psum x1, blocking collectives, local(): update = lax.psum(local_update, 'language')  28.4 us
    psum x1, blocking collectives, local(): total = lax.psum(jnp.sum(slot_grad, axis=1), 'language')  27.2 us
  transfers between devices with their start and end apart: 1, of which 1 were waited for; matrix products, arithmetic and copies ran while one was open for 0% of the time, Pallas kernels for 0%

commit v1 on v0

--- a/solution.py
+++ b/solution.py
@@ -4,6 +4,7 @@
 from jax.sharding import PartitionSpec as P
 
 STEP = 100
+do_views = lambda vector: lax.psum(lax.psum(vector, "fsdp"), "language")
 
 
 def log_weights(by_lang, square, old_weights):
@@ -25,7 +26,7 @@
     leader = (lax.axis_index("language") == 0).astype(jnp.float32)
     square_part = jnp.sum(total * total) * leader
     by_lang_part = jnp.dot(dots, onehot, precision=lax.Precision.HIGHEST)
-    by_lang, square = lax.psum((by_lang_part, square_part), ("language", "fsdp"))
+    by_lang, square = do_views((by_lang_part, square_part))
     new_logweights = log_weights(by_lang, square, old_weights)
     weights = jnp.exp(new_logweights)
     slot_weight = jnp.dot(onehot, weights, precision=lax.Precision.HIGHEST)

time: 506 us -> 579 us (1.14)
  the two profiles are of different devices: /device:TPU:2 before, /device:TPU:8 now
where the time goes in v1:
time: 579 us; the launch traced here: 578 us
  waiting for transfers between devices  326 us (56%)
  blocking collectives  224 us (39%)
  between operations  16.1 us (3%)
  local copies, waits for them, and re-layouts  5.81 us (1%)
    unnamed x2, waiting for transfers between devices  326 us
    psum x2, blocking collectives, do_views = lambda vector: lax.psum(lax.psum(vector, 'fsdp'), 'language')  169 us
    psum x1, blocking collectives, local(): update = lax.psum(local_update, 'language')  27.9 us
    psum x1, blocking collectives, local(): total = lax.psum(jnp.sum(slot_grad, axis=1), 'language')  27.2 us
  transfers between devices with their start and end apart: 1, of which 1 were waited for; matrix products, arithmetic and copies ran while one was open for 0% of the time, Pallas kernels for 0%

profile of v1, /device:TPU:8, one launch (start us, length us, event | category | flops | bytes accessed | tf_op | source)
XLA Modules:
  0.0 578.2 jit_solution(17938256195887167453)
XLA Ops:
  7.2 0.0 copy-start
  7.2 0.0 reduce-scatter.4.cloned.1.call-start
  7.2 1.7 copy-done
  8.9 2.8 fusion.7
  11.7 3.2 copy.16
  14.9 0.0 copy-start.5
  14.9 0.0 copy-start.4
  14.9 0.0 copy-start.1
  14.9 0.0 copy-start.2
  14.9 0.0 copy-start.3
  14.9 0.0 reduce-scatter.4.cloned.1.call-update
  15.0 325.9 %reduce-scatter.4.cloned.1.call-done = f32[80,128]{1,0:T(8,128)} async-done(((f32[5120,128]{1,0:T(8,128)}), f32[80,128]{1,0:T(8,128)}) %reduce-scatter.4.cloned.1.call-update) | async-done | bytes 40976
  340.9 0.9 copy.17
  341.8 27.2 %psum.42 = f32[80,64]{0,1:T(8,128)S(1)} all-reduce(f32[80,64]{0,1:T(8,128)S(1)} %reduce_sum.27), channel_id=1, replica_groups=mesh['language'=8,'fsdp'=64] {'language'}, use_global_device_ids=true, to_apply=%region_2.0 | all-reduce | flops 5120 | bytes 40960 | tf_op jit(solution)/shard_map/psum | solution.py:24
  369.0 0.6 multiply_reduce_fusion
  369.6 0.7 convolution_bitcast_fusion.2
  370.3 0.0 copy-done.5
  370.3 0.2 convolution_bitcast_fusion.1
  371.1 154.2 %all-reduce = (f32[16]{0:T(128)S(1)}, f32[]{:T(128)}) all-reduce(f32[16]{0:T(128)S(1)} %convolution_bitcast_fusion.1, f32[]{:T(128)S(6)} %mul.45), channel_id=1, replica_groups=mesh['language'=8,'fsdp'=64] {'fsdp'}, use_global_device_ids=true, to_apply=%region_3.0 | all-reduce | flops 17 | bytes 136 | tf_op jit(solution)/shard_map/psum | solution.py:7
  525.4 14.8 %all-reduce.1 = (f32[16]{0:T(128)S(1)}, f32[]{:T(128)}) all-reduce(f32[16]{0:T(128)S(1)} %get-tuple-element.4, f32[]{:T(128)} %get-tuple-element.5), channel_id=1, replica_groups=mesh['language'=8,'fsdp'=64] {'language'}, use_global_device_ids=true, to_apply=%region_4.0 | all-reduce | flops 17 | bytes 136 | tf_op jit(solution)/shard_map/psum | solution.py:7
  540.9 0.0 copy-done.4
  540.9 0.6 exponential_reduce_fusion
  542.2 0.0 copy-start.6
  542.2 0.2 convolution_bitcast_fusion
  542.4 0.4 fusion
  542.8 27.9 %psum.47 = f32[80,64]{0,1:T(8,128)S(1)} all-reduce(f32[80,64]{0,1:T(8,128)S(1)} %bitcast.34), channel_id=1, replica_groups=mesh['language'=8,'fsdp'=64] {'language'}, use_global_device_ids=true, to_apply=%region_9.0 | all-reduce | flops 5120 | bytes 40960 | tf_op jit(solution)/shard_map/psum | solution.py:34
  570.7 0.0 copy-done.1
  570.7 0.0 copy-done.2
  570.7 0.0 copy-done.3
  570.7 0.7 multiply_subtract_fusion
  571.4 0.0 copy-done.6
  (2 shorter events, 0.0 us)
Async XLA Ops:
  7.2 1.7 copy-start
  7.2 333.7 %reduce-scatter.4.cloned.1.call-start = ((), (), s32[]{:S(2)}) async-start(), calls=%async_computation.1 | async-start | bytes 2662400
  14.9 355.3 %copy-start.5 = (s32[2]{0:T(128)S(1)}, s32[2]{0:T(128)}, u32[]{:S(2)}) copy-start(s32[2]{0:T(128)} %param.9) | copy-start | bytes 28
  14.9 525.9 %copy-start.4 = (f32[16]{0:T(128)S(1)}, f32[16]{0:T(128)}, u32[]{:S(2)}) copy-start(f32[16]{0:T(128)} %param.10) | copy-start | bytes 196
  14.9 555.8 %copy-start.1 = (f32[80,64]{0,1:T(8,128)S(1)}, f32[80,64]{0,1:T(8,128)}, u32[]{:S(2)}) copy-start(f32[80,64]{0,1:T(8,128)} %param.11) | copy-start | bytes 61444
  14.9 555.8 %copy-start.2 = (f32[80,64]{0,1:T(8,128)S(1)}, f32[80,64]{0,1:T(8,128)}, u32[]{:S(2)}) copy-start(f32[80,64]{0,1:T(8,128)} %param.12) | copy-start | bytes 61444
  14.9 555.8 %copy-start.3 = (f32[80,64]{0,1:T(8,128)S(1)}, f32[80,64]{0,1:T(8,128)}, u32[]{:S(2)}) copy-start(f32[80,64]{0,1:T(8,128)} %param.13) | copy-start | bytes 61444
  542.2 29.2 %copy-start.6 = (f32[16]{0:T(128)}, f32[16]{0:T(128)S(1)}, u32[]{:S(2)}) copy-start(f32[16]{0:T(128)S(1)} %broadcast_subtract_fusion) | copy-start | bytes 196
Sparse Core Ops, SparseCore 0:
  15.1 325.7 reduce-scatter.3
